TPU v7x, 512 devices: a whole 4x8x8 slice. The times are simulated.
512 devices in a mesh: seq: 32 (over y, x), head: 2 (over core), expert: 8 (over z).
Axes of the slice: x: 4, y: 8, z: 8, core: 2. Of those that a mesh axis runs over, the one named last changes fastest.
Arguments:
- query_proj: bfloat16 [8, 4096, 2048], P('expert', 'seq', 'head'), may hold values from -6 to 6
- key_proj: bfloat16 [8, 4096, 2048], P('expert', 'seq', 'head'), may hold values from -6 to 6
- value_proj: bfloat16 [8, 4096, 2048], P('expert', 'seq', 'head'), may hold values from -6 to 6
- init_state: float32 [8, 16, 128, 128], P('expert', 'head'), may hold values from -384 to 384
- residual: bfloat16 [8, 4096, 2048], P('expert', ('seq', 'head')), may hold values from -6 to 6
- out_gain: float32 [2048], P('head'), may hold values from 0.1 to 1.9
- proj_weight: bfloat16 [2048, 2048], P('head', 'expert'), may hold values from -0.125 to 0.125
- moe_gain: float32 [2048], replicated, may hold values from 0.1 to 1.9
- w_gate: bfloat16 [64, 704, 2048], P(('seq', 'head'), None, 'expert'), may hold values from -0.125 to 0.125
- w_up: bfloat16 [64, 704, 2048], P(('seq', 'head'), None, 'expert'), may hold values from -0.125 to 0.125
- w_down: bfloat16 [64, 704, 2048], P(('seq', 'head'), None, 'expert'), may hold values from -0.21875 to 0.21875
- expert_ids: int32 [8, 4096, 6], P('expert', ('seq', 'head')), may hold values from 0 to 63, all different within a row; in each aligned block of 64 rows (0 to 63, 64 to 127, ..., all dimensions but the last counted through in order) at most 8 rows name the same one
- gate_weights: float32 [8, 4096, 6], P('expert', ('seq', 'head')), may hold values from 0.05 to 0.5
Outputs:
- layer_out: bfloat16 [8, 4096, 2048], P('expert', ('seq', 'head'))
Inputs may be any that keep to these rules, and one draw needn't show every extreme that they name: `expert_ids`: each token names 6 different experts. Among the 64 tokens of one device (aligned blocks of 64 positions) no expert is named more than 8 times, a bound that some block reaches.
All inputs are finite; a program needn't handle non-finite values.
Results may differ from a plain program's by a relative error of at most 0.019.
Values may be sent and summed in bfloat16 or wider, within the bound.
A program may use at most 128 MiB of HBM per device.

v0:
```python
import jax
import jax.numpy as jnp
from jax import lax
from jax.sharding import PartitionSpec as P

D = 2048
HD = 128
TOP = 6
HIGHEST = lax.Precision.HIGHEST


def carried_in(x, axis, join, neutral):
    place = lax.axis_index(axis)
    gathered = lax.all_gather(x.astype(jnp.bfloat16), axis)
    state = jnp.zeros_like(x) + jnp.asarray(neutral, x.dtype)

    def one(turn, state):
        return join(state, lax.dynamic_index_in_dim(gathered, turn, 0, False).astype(x.dtype))

    return lax.fori_loop(0, place, one, state)


def add_states(earlier, later):
    return earlier + later


def shards(
    query_proj,
    key_proj,
    value_proj,
    init_state,
    residual,
    out_gain,
    proj_weight,
    moe_gain,
    w_gate,
    w_up,
    w_down,
    expert_ids,
    gate_weights,
):
    tok_count = query_proj.shape[1]
    feat_width = query_proj.shape[2]
    head_count = feat_width // HD

    def to_heads(matrix):
        return matrix[0].astype(jnp.float32).reshape(tok_count, head_count, HD).transpose(1, 0, 2)

    query_heads = to_heads(query_proj)
    key_heads = to_heads(key_proj)
    value_heads = to_heads(value_proj)
    local_state = jnp.einsum("hsd,hse->hde", key_heads, value_heads, precision=HIGHEST)
    scanned = carried_in(local_state, "seq", add_states, jnp.zeros_like(local_state))
    prior_state = init_state[0] + scanned
    causal = jnp.tril(jnp.ones((tok_count, tok_count), jnp.float32))
    scores = jnp.einsum("htd,hsd->hts", query_heads, key_heads, precision=HIGHEST) * causal
    attended = jnp.einsum("hts,hsd->htd", scores, value_heads, precision=HIGHEST)
    attended = attended + jnp.einsum("htd,hde->hte", query_heads, prior_state, precision=HIGHEST)
    inv_norm = lax.rsqrt(jnp.mean(attended * attended, axis=-1, keepdims=True) + 1e-05)
    mixed = (
        (attended * inv_norm).transpose(1, 0, 2).reshape(tok_count, feat_width) * out_gain
    ).astype(jnp.bfloat16)
    row_count = residual.shape[1]
    wo_full, gate_full, up_full, down_full = (
        lax.all_gather(proj_weight, "expert", axis=1, tiled=True),
        lax.all_gather(w_gate, "expert", axis=2, tiled=True),
        lax.all_gather(w_up, "expert", axis=2, tiled=True),
        lax.all_gather(w_down, "expert", axis=2, tiled=True),
    )
    projected = lax.psum_scatter(
        jnp.dot(mixed, wo_full, preferred_element_type=jnp.float32).astype(jnp.bfloat16),
        "head",
        scatter_dimension=0,
        tiled=True,
    ).astype(jnp.float32)
    stream = (residual[0].astype(jnp.float32) + projected).astype(jnp.bfloat16)
    stream_f = lax.optimization_barrier(stream).astype(jnp.float32)
    moe_in = (
        stream_f
        * lax.rsqrt(jnp.mean(stream_f * stream_f, axis=-1, keepdims=True) + 1e-06)
        * moe_gain
    ).astype(jnp.bfloat16)
    experts_all = w_gate.shape[0] * lax.axis_size(("seq", "head"))
    capacity = max(2, 4 * row_count * TOP // (3 * experts_all))
    chosen = expert_ids[0].reshape(-1)
    onehot = (chosen[:, None] == lax.broadcasted_iota(jnp.int32, (1, experts_all), 1)).astype(
        jnp.int32
    )
    position = jnp.sum((jnp.cumsum(onehot, axis=0) - 1) * onehot, axis=1)
    target = (chosen * capacity + position).reshape(row_count, TOP)
    slot_ids = lax.broadcasted_iota(jnp.int32, (experts_all * capacity, 1, 1), 0)
    placing = jnp.any(target[None, :, :] == slot_ids, axis=-1).astype(jnp.bfloat16)
    outgoing = jnp.dot(placing, moe_in, preferred_element_type=jnp.float32).astype(jnp.bfloat16)
    outgoing = outgoing.reshape(experts_all, capacity, D)
    incoming = lax.all_to_all(outgoing, ("seq", "head"), split_axis=0, concat_axis=1, tiled=True)
    gate_act = jnp.einsum("ehd,erd->ehr", gate_full, incoming, preferred_element_type=jnp.float32)
    up_act = jnp.einsum("ehd,erd->ehr", up_full, incoming, preferred_element_type=jnp.float32)
    hidden = (jax.nn.silu(gate_act) * up_act).astype(jnp.bfloat16)
    results = jnp.einsum(
        "ehr,ehd->erd", hidden, down_full, preferred_element_type=jnp.float32
    ).astype(jnp.bfloat16)
    returned = lax.all_to_all(results, ("seq", "head"), split_axis=1, concat_axis=0, tiled=True)
    gathered_rows = jnp.take(
        returned.reshape(experts_all * capacity, D), target.reshape(-1), axis=0
    )
    gathered_rows = gathered_rows.reshape(row_count, TOP, D)
    combined = jnp.sum(gate_weights[0][:, :, None] * gathered_rows.astype(jnp.float32), axis=1)
    return (stream_f + combined).astype(jnp.bfloat16)[None]


def solution(mesh):
    placed = (
        P("expert", "seq", "head"),
        P("expert", "seq", "head"),
        P("expert", "seq", "head"),
        P("expert", "head", None, None),
        P("expert", ("seq", "head"), None),
        P("head"),
        P("head", "expert"),
        P(),
        P(("seq", "head"), None, "expert"),
        P(("seq", "head"), None, "expert"),
        P(("seq", "head"), None, "expert"),
        P("expert", ("seq", "head"), None),
        P("expert", ("seq", "head"), None),
    )
    return jax.shard_map(
        shards,
        mesh=mesh,
        in_specs=placed,
        out_specs=P("expert", ("seq", "head"), None),
        check_vma=False,
    )
```

profile of v0, /device:TPU:2, one launch (start us, length us, event | category | flops | bytes accessed | tf_op | source)
XLA Modules:
  0.0 490.9 jit_solution(9989508836682642384)
XLA Ops:
  6.5 1.0 copy.95
  7.6 1.1 copy.88
  8.7 0.9 convolution_convert_fusion.3
  9.7 0.7 all-gather.7.cloned.1.call-update
  10.5 0.2 convolution_multiply_fusion
  10.8 106.6 %all-gather.15.cloned.1.call-done = bf16[256,128,128]{2,1,0:T(8,128)(2,1)} async-done(((bf16[8,128,128]{2,1,0:T(8,128)(2,1)}), bf16[256,128,128]{2,1,0:T(8,128)(2,1)}) %all-gather.15.cloned.1.call-update) | async-done | bytes 8388624 | tf_op jit(solution)/shard_map/all_gather | solution.py:14
  117.5 1.2 while.10
  117.5 1.1 convert_add_fusion.4
  118.6 0.6 fusion.46
  119.2 0.7 fusion.44
  120.0 0.2 fusion.42
  120.3 63.5 %all-gather.7.cloned.1.call-done = bf16[1024,2048]{1,0:T(8,128)(2,1)} async-done(((bf16[1024,256]{1,0:T(8,128)(2,1)}), bf16[1024,2048]{1,0:T(8,128)(2,1)}) %all-gather.7.cloned.1.call-update) | async-done | bytes 4194320 | tf_op jit(solution)/shard_map/all_gather | solution.py:65
  183.8 3.8 convolution_convert_fusion.2
  187.6 0.5 all-gather.9.cloned.1.call-update
  188.2 0.5 all-gather.11.cloned.1.call-update
  188.8 0.5 all-gather.13.cloned.1.call-update
  189.4 0.1 eq.41
  189.5 0.1 reshape_squeeze.3
  189.7 0.9 reduce-window.6
  190.6 0.2 slice_reduce_fusion
  190.9 0.1 fusion.60
  191.0 0.1 reduce_sum.45
  191.2 0.2 fusion.35
  191.4 10.7 %reduce-scatter.2.cloned.1.call-done = bf16[64,2048]{1,0:T(8,128)(2,1)} async-done(((bf16[128,2048]{1,0:T(8,128)(2,1)}), bf16[64,2048]{1,0:T(8,128)(2,1)}) %reduce-scatter.2.cloned.1.call-update) | async-done | bytes 262160 | tf_op jit(solution)/shard_map/reduce_scatter | solution.py:70
  202.1 1.0 fusion.41
  203.1 0.2 fusion.37
  203.3 2.2 fusion.5
  205.4 10.3 %all-to-all-start = ((bf16[64,8,2048]{2,1,0:T(8,128)(2,1)}), bf16[64,8,2048]{2,1,0:T(8,128)(2,1)S(1)}, u32[]{:S(2)}, u32[]{:S(2)}) async-start(bf16[64,8,2048]{2,1,0:T(8,128)(2,1)} %fusion.5), calls=%async_computation.1 | async-start | bytes 4194304 | tf_op jit(solution)/shard_map/all_to_all | solution.py:95
  215.7 45.4 %all-gather.9.cloned.1.call-done = bf16[1,704,2048]{2,1,0:T(8,128)(2,1)} async-done(((bf16[1,704,256]{2,1,0:T(8,128)(2,1)}), bf16[1,704,2048]{2,1,0:T(8,128)(2,1)}) %all-gather.9.cloned.1.call-update) | async-done | bytes 2883600 | tf_op jit(solution)/shard_map/all_gather | solution.py:66
  261.1 5.8 %all-to-all-done = bf16[64,8,2048]{2,1,0:T(8,128)(2,1)S(1)} async-done(((bf16[64,8,2048]{2,1,0:T(8,128)(2,1)}), bf16[64,8,2048]{2,1,0:T(8,128)(2,1)S(1)}, u32[]{:S(2)}, u32[]{:S(2)}) %all-to-all-start) | async-done | bytes 2097184 | tf_op jit(solution)/shard_map/all_to_all | solution.py:95
  267.0 5.4 %fusion.11 = f32[704,512]{1,0:T(8,128)} fusion(bf16[1,704,2048]{2,1,0:T(8,128)(2,1)} %all-gather.9.cloned.1.call-done, bf16[64,8,2048]{2,1,0:T(8,128)(2,1)S(1)} %all-to-all-done), kind=kOutput, calls=%fused_computation.16 | convolution fusion | flops 1476395008 | bytes 6422528 | tf_op jit(solution)/shard_map/ehd,erd->ehr/dot_general | solution.py:96
  272.3 45.2 %all-gather.11.cloned.1.call-done = bf16[1,704,2048]{2,1,0:T(8,128)(2,1)} async-done(((bf16[1,704,256]{2,1,0:T(8,128)(2,1)}), bf16[1,704,2048]{2,1,0:T(8,128)(2,1)}) %all-gather.11.cloned.1.call-update) | async-done | bytes 2883600 | tf_op jit(solution)/shard_map/all_gather | solution.py:67
  317.5 56.4 %all-gather.13.cloned.1.call-done = bf16[1,704,2048]{2,1,0:T(8,128)(2,1)} async-done(((bf16[1,704,256]{2,1,0:T(8,128)(2,1)}), bf16[1,704,2048]{2,1,0:T(8,128)(2,1)}) %all-gather.13.cloned.1.call-update) | async-done | bytes 2883600 | tf_op jit(solution)/shard_map/all_gather | solution.py:68
  374.0 7.2 %fusion.6 = bf16[1,512,2048]{2,1,0:T(8,128)(2,1)S(1)} fusion(bf16[1,704,2048]{2,1,0:T(8,128)(2,1)} %all-gather.13.cloned.1.call-done, bf16[1,704,2048]{2,1,0:T(8,128)(2,1)} %all-gather.11.cloned.1.call-done, bf16[64,8,2048]{2,1,0:T(8,128)(2,1)} %copy-done, f32[704,512]{1,0:T(8,128)} %fusion.11), kind=kOutput, calls=%fused_computation.11 | convolution fusion | flops 2956001280 | bytes 11403264 | tf_op jit(solution)/shard_map/ehr,ehd->erd/dot_general | solution.py:99
  381.1 5.2 %copy.121 = bf16[1,512,2048]{2,0,1:T(2,128)(2,1)} copy(bf16[1,512,2048]{2,1,0:T(8,128)(2,1)S(1)} %fusion.6) | data formatting | bytes 4194304 | tf_op jit(solution)/shard_map/convert_element_type | solution.py:101
  386.3 0.5 broadcast.124
  386.8 13.2 %reduce.4 = bf16[512,2048]{1,0:T(8,128)(2,1)S(1)} reduce(bf16[512,1,2048]{2,1,0:T(2,128)(2,1)} %bitcast.140, bf16[]{:T(256)} %broadcast.124), dimensions={1}, to_apply=%bitcast.135.reduce_sub_computation | reduce | bytes 4194306
  400.0 3.3 reshape.176
  403.3 10.4 %all-to-all-start.1 = ((bf16[64,2,8192]{2,1,0:T(2,128)(2,1)}), bf16[64,2,8192]{2,1,0:T(2,128)(2,1)S(1)}, u32[]{:S(2)}, u32[]{:S(2)}) async-start(bf16[64,2,8192]{2,1,0:T(2,128)(2,1)} %reshape.176), calls=%async_computation.2 | async-start | bytes 4194304 | tf_op jit(solution)/shard_map/all_to_all | solution.py:102
  413.7 0.1 reduce_sum.44
  413.9 0.1 mul.112
  414.4 50.5 %all-to-all-done.1 = bf16[64,2,8192]{2,1,0:T(2,128)(2,1)S(1)} async-done(((bf16[64,2,8192]{2,1,0:T(2,128)(2,1)}), bf16[64,2,8192]{2,1,0:T(2,128)(2,1)S(1)}, u32[]{:S(2)}, u32[]{:S(2)}) %all-to-all-start.1) | async-done | bytes 2097184 | tf_op jit(solution)/shard_map/all_to_all | solution.py:102
  464.9 6.8 %reshape.177 = bf16[512,1,2048]{2,1,0:T(2,128)(2,1)} reshape(bf16[64,2,8192]{2,1,0:T(2,128)(2,1)S(1)} %all-to-all-done.1) | data formatting | bytes 4194304
  471.7 3.5 copy.120
  475.2 3.1 gather_fusion
  478.3 2.5 gather.7
  480.8 2.5 multiply_reduce_fusion
  483.3 0.8 fusion.47
  (42 shorter events, 1.1 us)
Async XLA Ops:
  6.5 3.9 copy-start.3
  6.5 110.9 %all-gather.15.cloned.1.call-start = ((), (), s32[]{:S(2)}) async-start(), calls=%async_computation.8 | async-start | bytes 8650752 | tf_op jit(solution)/shard_map/all_gather | solution.py:14
  9.7 174.1 %all-gather.7.cloned.1.call-start = ((), (), s32[]{:S(2)}) async-start(), calls=%async_computation.3 | async-start | bytes 4718592 | tf_op jit(solution)/shard_map/all_gather | solution.py:65
  10.4 191.7 %reduce-scatter.2.cloned.1.call-start = ((), (), s32[]{:S(2)}) async-start(), calls=%async_computation.4 | async-start | bytes 786432 | tf_op jit(solution)/shard_map/reduce_scatter | solution.py:70
  117.4 1.2 copy-start.1
  119.2 0.8 copy-start.6
  120.3 69.0 %copy-start.4 = (s32[1,64,6]{1,0,2:T(1,128)S(1)}, s32[1,64,6]{1,0,2:T(1,128)}, u32[]{:S(2)}) copy-start(s32[1,64,6]{1,0,2:T(1,128)} %param.26) | copy-start | bytes 4612
  187.5 14.5 %copy-start.2 = (bf16[1,64,2048]{2,1,0:T(8,128)(2,1)S(1)}, bf16[1,64,2048]{2,1,0:T(8,128)(2,1)}, u32[]{:S(2)}) copy-start(bf16[1,64,2048]{2,1,0:T(8,128)(2,1)} %param.19) | copy-start | bytes 786436
  187.5 15.7 %copy-start.5 = (f32[2048]{0:T(1024)S(1)}, f32[2048]{0:T(1024)}, u32[]{:S(2)}) copy-start(f32[2048]{0:T(1024)} %param.22) | copy-start | bytes 24580
  187.5 73.6 %all-gather.9.cloned.1.call-start = ((), (), s32[]{:S(2)}) async-start(), calls=%async_computation.5 | async-start | bytes 3244032 | tf_op jit(solution)/shard_map/all_gather | solution.py:66
  188.1 129.4 %all-gather.11.cloned.1.call-start = ((), (), s32[]{:S(2)}) async-start(), calls=%async_computation.6 | async-start | bytes 3244032 | tf_op jit(solution)/shard_map/all_gather | solution.py:67
  188.7 185.2 %all-gather.13.cloned.1.call-start = ((), (), s32[]{:S(2)}) async-start(), calls=%async_computation.7 | async-start | bytes 3244032 | tf_op jit(solution)/shard_map/all_gather | solution.py:68
  205.4 61.5 %all-to-all-start = ((bf16[64,8,2048]{2,1,0:T(8,128)(2,1)}), bf16[64,8,2048]{2,1,0:T(8,128)(2,1)S(1)}, u32[]{:S(2)}, u32[]{:S(2)}) async-start(bf16[64,8,2048]{2,1,0:T(8,128)(2,1)} %fusion.5), calls=%async_computation.1 | async-start | bytes 4194304 | tf_op jit(solution)/shard_map/all_to_all | solution.py:95
  266.9 5.4 %copy-start = (bf16[64,8,2048]{2,1,0:T(8,128)(2,1)}, bf16[64,8,2048]{2,1,0:T(8,128)(2,1)S(1)}, u32[]{:S(2)}) copy-start(bf16[64,8,2048]{2,1,0:T(8,128)(2,1)S(1)} %all-to-all-done) | copy-start | bytes 6291460
  403.3 11.0 %copy-start.7 = (f32[1,64,6]{1,0,2:T(1,128)S(1)}, f32[1,64,6]{1,0,2:T(1,128)}, u32[]{:S(2)}) copy-start(f32[1,64,6]{1,0,2:T(1,128)} %param.27) | copy-start | bytes 4612
  403.3 61.7 %all-to-all-start.1 = ((bf16[64,2,8192]{2,1,0:T(2,128)(2,1)}), bf16[64,2,8192]{2,1,0:T(2,128)(2,1)S(1)}, u32[]{:S(2)}, u32[]{:S(2)}) async-start(bf16[64,2,8192]{2,1,0:T(2,128)(2,1)} %reshape.176), calls=%async_computation.2 | async-start | bytes 4194304 | tf_op jit(solution)/shard_map/all_to_all | solution.py:102
Sparse Core Ops, SparseCore 0:
  10.5 106.8 all-gather.14
  119.4 64.3 all-gather.6
  187.7 14.3 reduce-scatter.1
  204.1 56.9 all-gather.8
  263.2 54.3 all-gather.10
  319.6 54.3 all-gather.12
where the time goes:
time: 492 us; the launch traced here: 491 us
  waiting for transfers between devices  387 us (79%)
  local copies, waits for them, and re-layouts  28.5 us (6%)
  starting transfers between devices  20.9 us (4%)
  matrix products  20.9 us (4%)
  other arithmetic  20.3 us (4%)
  between operations  13.7 us (3%)
    all_gather x1, waiting for transfers between devices, carried_in(): gathered = lax.all_gather(x.astype(jnp.bfloat16), axis)  107 us
    all_gather x1, waiting for transfers between devices, shards(): lax.all_gather(proj_weight, 'expert', axis=1, tiled=True)  63.5 us
    all_gather x1, waiting for transfers between devices, shards(): lax.all_gather(w_down, 'expert', axis=2, tiled=True)  56.4 us
    all_to_all x1, waiting for transfers between devices, shards(): lax.all_to_all(results, ('seq', 'head'), split_axis=1, concat_axis=0, til...  50.5 us
    all_gather x1, waiting for transfers between devices, shards(): lax.all_gather(w_gate, 'expert', axis=2, tiled=True)  45.4 us
    all_gather x1, waiting for transfers between devices, shards(): lax.all_gather(w_up, 'expert', axis=2, tiled=True)  45.2 us
    unnamed x23, local copies, waits for them, and re-layouts  15.2 us
    unnamed x1, other arithmetic  13.2 us
  transfers between devices with their start and end apart: 8, of which 8 were waited for; matrix products, arithmetic and copies ran while one was open for 3% of the time, Pallas kernels for 0%

commit v1 on v0

--- a/solution.py
+++ b/solution.py
@@ -7,6 +7,13 @@
 HD = 128
 TOP = 6
 HIGHEST = lax.Precision.HIGHEST
+
+
+def gather_over(x, name, dim):
+    n_dev = lax.axis_size(name)
+    blocks = jnp.stack([x for _ in range(n_dev)])
+    blocks = lax.all_to_all(blocks, name, split_axis=0, concat_axis=0)
+    return jnp.concatenate(blocks, axis=dim)
 
 
 def carried_in(x, axis, join, neutral):
@@ -65,7 +72,7 @@
         lax.all_gather(proj_weight, "expert", axis=1, tiled=True),
         lax.all_gather(w_gate, "expert", axis=2, tiled=True),
         lax.all_gather(w_up, "expert", axis=2, tiled=True),
-        lax.all_gather(w_down, "expert", axis=2, tiled=True),
+        gather_over(w_down, "expert", 2),
     )
     projected = lax.psum_scatter(
         jnp.dot(mixed, wo_full, preferred_element_type=jnp.float32).astype(jnp.bfloat16),

time: 492 us -> 468 us (0.951)
  waiting for transfers between devices: 387 us -> 352 us
  local copies, waits for them, and re-layouts: 28.5 us -> 33.9 us
    all_to_all x0 -> x1, waiting for transfers between devices: none -> 67.3 us  [gather_over(): blocks = lax.all_to_all(blocks, name, split_axis=0, concat_axis=0)]
    all_gather x1 -> x0, waiting for transfers between devices: 56.4 us -> none  [shards(): lax.all_gather(w_down, 'expert', axis=2, tiled=True)]
    all_gather x1, waiting for transfers between devices: 45.4 us -> 5.42 us  [shards(): lax.all_gather(w_gate, 'expert', axis=2, tiled=True)]
    all_to_all x1, waiting for transfers between devices: 5.83 us -> 43.8 us  [shards(): lax.all_to_all(outgoing, ('seq', 'head'), split_axis=0, concat_axis=1, ti...]
    all_gather x1, waiting for transfers between devices: 45.2 us -> 7.99 us  [shards(): lax.all_gather(w_up, 'expert', axis=2, tiled=True)]
    reduce_scatter x1, waiting for transfers between devices: 10.7 us -> 4.94 us  [shards(): lax.psum_scatter(jnp.dot(mixed, wo_full, preferred_element_type=jnp.float...]
    unnamed x23 -> x26, local copies, waits for them, and re-layouts: 15.2 us -> 17.2 us
  transfers between devices with their start and end apart: 8 -> 8, of which waited for: 8 -> 8; matrix products, arithmetic and copies ran while one was open for 3% -> 4% of each run, Pallas kernels for 0% -> 0%
where the time goes in v1:
time: 468 us; the launch traced here: 466 us
  waiting for transfers between devices  352 us (75%)
  local copies, waits for them, and re-layouts  33.9 us (7%)
  starting transfers between devices  25.5 us (5%)
  matrix products  21.2 us (5%)
  other arithmetic  20.3 us (4%)
  between operations  13.4 us (3%)
    all_gather x1, waiting for transfers between devices, carried_in(): gathered = lax.all_gather(x.astype(jnp.bfloat16), axis)  107 us
    all_to_all x1, waiting for transfers between devices, gather_over(): blocks = lax.all_to_all(blocks, name, split_axis=0, concat_axis=0)  67.3 us
    all_gather x1, waiting for transfers between devices, shards(): lax.all_gather(proj_weight, 'expert', axis=1, tiled=True)  63.5 us
    all_to_all x1, waiting for transfers between devices, shards(): lax.all_to_all(results, ('seq', 'head'), split_axis=1, concat_axis=0, til...  50.5 us
    all_to_all x1, waiting for transfers between devices, shards(): lax.all_to_all(outgoing, ('seq', 'head'), split_axis=0, concat_axis=1, ti...  43.8 us
    unnamed x26, local copies, waits for them, and re-layouts  17.2 us
    unnamed x1, other arithmetic  13.2 us
    all_to_all x1, starting transfers between devices, shards(): lax.all_to_all(results, ('seq', 'head'), split_axis=1, concat_axis=0, til...  10.4 us
  transfers between devices with their start and end apart: 8, of which 8 were waited for; matrix products, arithmetic and copies ran while one was open for 4% of the time, Pallas kernels for 0%

profile of v1, /device:TPU:2, one launch (start us, length us, event | category | flops | bytes accessed | tf_op | source)
XLA Modules:
  0.0 466.2 jit_solution(14239424978762427852)
XLA Ops:
  6.5 1.0 copy.99
  7.6 1.1 copy.92
  8.7 0.9 convolution_convert_fusion.3
  9.7 0.7 all-gather.6.cloned.1.call-update
  10.5 0.2 convolution_multiply_fusion
  10.8 106.6 %all-gather.12.cloned.1.call-done = bf16[256,128,128]{2,1,0:T(8,128)(2,1)} async-done(((bf16[8,128,128]{2,1,0:T(8,128)(2,1)}), bf16[256,128,128]{2,1,0:T(8,128)(2,1)}) %all-gather.12.cloned.1.call-update) | async-done | bytes 8388624 | tf_op jit(solution)/shard_map/all_gather | solution.py:21
  117.5 1.2 while.10
  117.5 1.1 convert_add_fusion.4
  118.6 0.6 fusion.43
  119.2 0.7 fusion.41
  120.0 0.2 fusion.39
  120.3 63.5 %all-gather.6.cloned.1.call-done = bf16[1024,2048]{1,0:T(8,128)(2,1)} async-done(((bf16[1024,256]{1,0:T(8,128)(2,1)}), bf16[1024,2048]{1,0:T(8,128)(2,1)}) %all-gather.6.cloned.1.call-update) | async-done | bytes 4194320 | tf_op jit(solution)/shard_map/all_gather | solution.py:72
  183.8 3.8 convolution_convert_fusion.2
  187.6 0.5 all-gather.8.cloned.1.call-update
  188.1 1.8 stack.2
  189.9 4.5 all-to-all-start.1
  194.5 0.5 all-gather.10.cloned.1.call-update
  195.1 0.1 eq.41
  195.3 0.1 reshape_squeeze.3
  195.4 0.9 reduce-window.6
  196.3 0.2 slice_reduce_fusion
  196.7 0.1 reduce_sum.45
  196.9 0.2 fusion.32
  197.1 4.9 %reduce-scatter.2.cloned.1.call-done = bf16[64,2048]{1,0:T(8,128)(2,1)} async-done(((bf16[128,2048]{1,0:T(8,128)(2,1)}), bf16[64,2048]{1,0:T(8,128)(2,1)}) %reduce-scatter.2.cloned.1.call-update) | async-done | bytes 262160 | tf_op jit(solution)/shard_map/reduce_scatter | solution.py:77
  202.1 1.0 fusion.38
  203.1 0.2 fusion.34
  203.3 2.1 fusion.4
  205.4 67.3 %all-to-all-done.1 = bf16[8,1,704,256]{3,2,1,0:T(8,128)(2,1)S(1)} async-done(((bf16[8,1,704,256]{3,2,1,0:T(8,128)(2,1)}), bf16[8,1,704,256]{3,2,1,0:T(8,128)(2,1)S(1)}, u32[]{:S(2)}, u32[]{:S(2)}) %all-to-all-start.1) | async-done | bytes 2883616 | tf_op jit(solution)/shard_map/all_to_all | solution.py:15
  272.7 10.4 %all-to-all-start = ((bf16[64,8,2048]{2,1,0:T(8,128)(2,1)}), bf16[64,8,2048]{2,1,0:T(8,128)(2,1)}, u32[]{:S(2)}, u32[]{:S(2)}) async-start(bf16[64,8,2048]{2,1,0:T(8,128)(2,1)} %fusion.4), calls=%async_computation.1 | async-start | bytes 4194304 | tf_op jit(solution)/shard_map/all_to_all | solution.py:102
  283.1 2.0 copy.100
  285.1 5.4 %all-gather.8.cloned.1.call-done = bf16[1,704,2048]{2,1,0:T(8,128)(2,1)} async-done(((bf16[1,704,256]{2,1,0:T(8,128)(2,1)}), bf16[1,704,2048]{2,1,0:T(8,128)(2,1)}) %all-gather.8.cloned.1.call-update) | async-done | bytes 2883600 | tf_op jit(solution)/shard_map/all_gather | solution.py:73
  290.5 43.8 %all-to-all-done = bf16[64,8,2048]{2,1,0:T(8,128)(2,1)} async-done(((bf16[64,8,2048]{2,1,0:T(8,128)(2,1)}), bf16[64,8,2048]{2,1,0:T(8,128)(2,1)}, u32[]{:S(2)}, u32[]{:S(2)}) %all-to-all-start) | async-done | bytes 2097184 | tf_op jit(solution)/shard_map/all_to_all | solution.py:102
  334.3 5.3 %fusion.8 = f32[704,512]{1,0:T(8,128)} fusion(bf16[1,704,2048]{2,1,0:T(8,128)(2,1)} %all-gather.8.cloned.1.call-done, bf16[64,8,2048]{2,1,0:T(8,128)(2,1)} %all-to-all-done), kind=kOutput, calls=%fused_computation.15 | convolution fusion | flops 1476395008 | bytes 6422528 | tf_op jit(solution)/shard_map/ehd,erd->ehr/dot_general | solution.py:103
  339.5 8.0 %all-gather.10.cloned.1.call-done = bf16[1,704,2048]{2,1,0:T(8,128)(2,1)} async-done(((bf16[1,704,256]{2,1,0:T(8,128)(2,1)}), bf16[1,704,2048]{2,1,0:T(8,128)(2,1)}) %all-gather.10.cloned.1.call-update) | async-done | bytes 2883600 | tf_op jit(solution)/shard_map/all_gather | solution.py:74
  347.5 7.6 %fusion.5 = bf16[1,512,2048]{2,1,0:T(8,128)(2,1)} fusion(bf16[704,2048]{1,0:T(8,128)(2,1)S(1)} %bitcast.146, bf16[1,704,2048]{2,1,0:T(8,128)(2,1)} %all-gather.10.cloned.1.call-done, bf16[64,8,2048]{2,1,0:T(8,128)(2,1)} %all-to-all-done, f32[704,512]{1,0:T(8,128)} %fusion.8), kind=kOutput, calls=%fused_computation.10 | convolution fusion | flops 2956001280 | bytes 11403264 | tf_op jit(solution)/shard_map/ehr,ehd->erd/dot_general | solution.py:106
  355.2 6.8 %copy.127 = bf16[1,512,2048]{2,0,1:T(2,128)(2,1)} copy(bf16[1,512,2048]{2,1,0:T(8,128)(2,1)} %fusion.5) | data formatting | bytes 4194304 | tf_op jit(solution)/shard_map/convert_element_type | solution.py:108
  361.9 0.5 broadcast.127
  362.5 13.2 %reduce.4 = bf16[512,2048]{1,0:T(8,128)(2,1)S(1)} reduce(bf16[512,1,2048]{2,1,0:T(2,128)(2,1)} %bitcast.143, bf16[]{:T(256)} %broadcast.127), dimensions={1}, to_apply=%bitcast.138.reduce_sub_computation | reduce | bytes 4194306
  375.6 3.3 reshape.185
  378.9 10.4 %all-to-all-start.2 = ((bf16[64,2,8192]{2,1,0:T(2,128)(2,1)}), bf16[64,2,8192]{2,1,0:T(2,128)(2,1)S(1)}, u32[]{:S(2)}, u32[]{:S(2)}) async-start(bf16[64,2,8192]{2,1,0:T(2,128)(2,1)} %reshape.185), calls=%async_computation.3 | async-start | bytes 4194304 | tf_op jit(solution)/shard_map/all_to_all | solution.py:109
  389.5 0.1 mul.112
  390.0 50.5 %all-to-all-done.2 = bf16[64,2,8192]{2,1,0:T(2,128)(2,1)S(1)} async-done(((bf16[64,2,8192]{2,1,0:T(2,128)(2,1)}), bf16[64,2,8192]{2,1,0:T(2,128)(2,1)S(1)}, u32[]{:S(2)}, u32[]{:S(2)}) %all-to-all-start.2) | async-done | bytes 2097184 | tf_op jit(solution)/shard_map/all_to_all | solution.py:109
  440.6 6.8 %reshape.186 = bf16[512,1,2048]{2,1,0:T(2,128)(2,1)} reshape(bf16[64,2,8192]{2,1,0:T(2,128)(2,1)S(1)} %all-to-all-done.2) | data formatting | bytes 4194304
  447.3 3.5 copy.126
  450.8 3.1 gather_fusion
  453.9 2.5 gather.7
  456.4 2.5 multiply_reduce_fusion
  458.9 0.8 fusion.44
  (45 shorter events, 1.3 us)
Async XLA Ops:
  6.5 3.9 copy-start.4
  6.5 110.9 %all-gather.12.cloned.1.call-start = ((), (), s32[]{:S(2)}) async-start(), calls=%async_computation.8 | async-start | bytes 8650752 | tf_op jit(solution)/shard_map/all_gather | solution.py:21
  9.7 174.1 %all-gather.6.cloned.1.call-start = ((), (), s32[]{:S(2)}) async-start(), calls=%async_computation.4 | async-start | bytes 4718592 | tf_op jit(solution)/shard_map/all_gather | solution.py:72
  10.4 191.6 %reduce-scatter.2.cloned.1.call-start = ((), (), s32[]{:S(2)}) async-start(), calls=%async_computation.5 | async-start | bytes 786432 | tf_op jit(solution)/shard_map/reduce_scatter | solution.py:77
  117.4 1.2 copy-start.1
  119.2 0.8 copy-start.7
  120.3 67.9 %copy-start.2 = (bf16[1,704,256]{2,1,0:T(8,128)(2,1)S(1)}, bf16[1,704,256]{2,1,0:T(8,128)(2,1)}, u32[]{:S(2)}) copy-start(bf16[1,704,256]{2,1,0:T(8,128)(2,1)} %param.25) | copy-start | bytes 1081348
  187.5 103.0 %all-gather.8.cloned.1.call-start = ((), (), s32[]{:S(2)}) async-start(), calls=%async_computation.6 | async-start | bytes 3244032 | tf_op jit(solution)/shard_map/all_gather | solution.py:73
  189.9 5.1 %copy-start.5 = (s32[1,64,6]{1,0,2:T(1,128)S(1)}, s32[1,64,6]{1,0,2:T(1,128)}, u32[]{:S(2)}) copy-start(s32[1,64,6]{1,0,2:T(1,128)} %param.26) | copy-start | bytes 4612
  189.9 12.2 %copy-start.3 = (bf16[1,64,2048]{2,1,0:T(8,128)(2,1)S(1)}, bf16[1,64,2048]{2,1,0:T(8,128)(2,1)}, u32[]{:S(2)}) copy-start(bf16[1,64,2048]{2,1,0:T(8,128)(2,1)} %param.19) | copy-start | bytes 786436
  189.9 82.8 %all-to-all-start.1 = ((bf16[8,1,704,256]{3,2,1,0:T(8,128)(2,1)}), bf16[8,1,704,256]{3,2,1,0:T(8,128)(2,1)S(1)}, u32[]{:S(2)}, u32[]{:S(2)}) async-start(bf16[8,1,704,256]{3,2,1,0:T(8,128)(2,1)} %stack.2), calls=%async_computation.2 | async-start | bytes 5767168 | tf_op jit(solution)/shard_map/all_to_all | solution.py:15
  194.4 8.8 %copy-start.6 = (f32[2048]{0:T(1024)S(1)}, f32[2048]{0:T(1024)}, u32[]{:S(2)}) copy-start(f32[2048]{0:T(1024)} %param.22) | copy-start | bytes 24580
  194.4 153.1 %all-gather.10.cloned.1.call-start = ((), (), s32[]{:S(2)}) async-start(), calls=%async_computation.7 | async-start | bytes 3244032 | tf_op jit(solution)/shard_map/all_gather | solution.py:74
  272.7 61.6 %all-to-all-start = ((bf16[64,8,2048]{2,1,0:T(8,128)(2,1)}), bf16[64,8,2048]{2,1,0:T(8,128)(2,1)}, u32[]{:S(2)}, u32[]{:S(2)}) async-start(bf16[64,8,2048]{2,1,0:T(8,128)(2,1)} %fusion.4), calls=%async_computation.1 | async-start | bytes 4194304 | tf_op jit(solution)/shard_map/all_to_all | solution.py:102
  285.1 62.4 %copy-start = (bf16[88,8,8,256]{3,1,2,0:T(8,128)(2,1)S(1)}, bf16[88,8,8,256]{3,1,2,0:T(8,128)(2,1)}, u32[]{:S(2)}) copy-start(bf16[88,8,8,256]{3,1,2,0:T(8,128)(2,1)} %copy.100) | copy-start | bytes 8650756
  378.9 11.0 %copy-start.8 = (f32[1,64,6]{1,0,2:T(1,128)S(1)}, f32[1,64,6]{1,0,2:T(1,128)}, u32[]{:S(2)}) copy-start(f32[1,64,6]{1,0,2:T(1,128)} %param.27) | copy-start | bytes 4612
  378.9 61.7 %all-to-all-start.2 = ((bf16[64,2,8192]{2,1,0:T(2,128)(2,1)}), bf16[64,2,8192]{2,1,0:T(2,128)(2,1)S(1)}, u32[]{:S(2)}, u32[]{:S(2)}) async-start(bf16[64,2,8192]{2,1,0:T(2,128)(2,1)} %reshape.185), calls=%async_computation.3 | async-start | bytes 4194304 | tf_op jit(solution)/shard_map/all_to_all | solution.py:109
Sparse Core Ops, SparseCore 0:
  10.5 106.8 all-gather.11
  119.4 64.3 all-gather.5
  187.7 14.3 reduce-scatter.1
  204.1 86.3 all-gather.7
  292.6 54.9 all-gather.9
